TPU v7x, 32 devices: a whole 2x2x4 slice. The times are simulated.
32 devices in a mesh: tile: 4 (over y, x), query: 2 (over core), dp: 4 (over z).
Axes of the slice: x: 2, y: 2, z: 4, core: 2. Of those that a mesh axis runs over, the one named last changes fastest.
Arguments:
- features: bfloat16 [4, 32768, 256], P('dp', ('tile', 'query')), may hold values from -6 to 6
- queries: bfloat16 [4, 64, 256], P('dp', ('tile', 'query')), may hold values from -6 to 6
- out_grad: bfloat16 [4, 64, 256], P('dp', ('tile', 'query')), may hold values from -48 to 48
- value_weight: bfloat16 [256, 256], replicated, may hold values from -0.375 to 0.375
- attn_weight: bfloat16 [256, 128], replicated, may hold values from -0.375 to 0.375
- out_weight: bfloat16 [256, 256], replicated, may hold values from -0.375 to 0.375
- slot_point: int32 [4, 16384], P('dp', ('tile', 'query')), may hold values from 0 to 8191, as said below
- slot_rows: int32 [4, 4, 16384], P('dp', None, ('tile', 'query')), may hold values from 0 to 4095, as said below
- slot_bilinear: float32 [4, 4, 16384], P('dp', None, ('tile', 'query')), may hold values from 0 to 1, as said below
- slot_count: int32 [4, 8], P('dp', ('tile', 'query')), may hold values from 1 to 2048, as said below
Outputs:
- feature_grad: bfloat16 [4, 32768, 256], P('dp', ('tile', 'query'))
- query_grad: bfloat16 [4, 64, 256], P('dp', ('tile', 'query'))
- value_weight_grad: float32 [256, 256], replicated
- attn_weight_grad: float32 [256, 128], replicated
- out_weight_grad: float32 [256, 256], replicated
Inputs may be any that keep to these rules, and one draw needn't show every extreme that they name: `slot_count`: per page one owner has exactly 2048 live slots; the counts of a page sum to 8192. `slot_point`: the live slots of a page name every sample point exactly once, point m = q * 128 + head * 4 * 4 + level * 4 + point; slots that are not live hold arbitrary point numbers. `slot_rows`: the corners of a slot are rows r, r + 1, r + 64, r + 65 of the owner's tokens laid out in lines of 64. `slot_bilinear`: the four weights of a slot sum to one.
All inputs are finite; a program needn't handle non-finite values.
Results may differ from a plain program's by a relative error of at most 0.0064.
Values may be sent and summed in bfloat16 or wider, within the bound.
A program may use at most 128 MiB of HBM per device.

v0:
```python
import jax
import jax.numpy as jnp
from jax import lax
from jax.sharding import PartitionSpec as P

HEADS = 8
TILE_W = 64


def over_rows(left, right):
    return lax.dot_general(
        left, right, (((0,), (0,)), ((), ())), preferred_element_type=jnp.float32
    )


def over_rows_exact(left, right):
    return lax.dot_general(
        left,
        right,
        (((0,), (0,)), ((), ())),
        precision=lax.Precision.HIGHEST,
        preferred_element_type=jnp.float32,
    )


def times_transpose(left, right):
    return lax.dot_general(
        left, right, (((1,), (1,)), ((), ())), preferred_element_type=jnp.float32
    )


def shift_down(block, offset):
    return jnp.concatenate(
        [jnp.zeros((offset, block.shape[1]), block.dtype), block[: block.shape[0] - offset]], axis=0
    )


def local(
    features,
    queries,
    out_grad,
    value_weight,
    attn_weight,
    out_weight,
    slot_point,
    slot_rows,
    slot_bilinear,
    slot_count,
):
    owners = lax.axis_size(("tile", "query"))
    page_count = lax.axis_size("dp")
    local_queries = queries.shape[1]
    all_queries = local_queries * owners
    grad_scale = float(page_count * all_queries) ** (-0.5)
    width = features.shape[2]
    att_width = attn_weight.shape[1]
    per_head = att_width // HEADS
    head_width = width // HEADS
    exponent = jnp.exp(
        jnp.dot(queries[0], attn_weight, preferred_element_type=jnp.float32)
    ).reshape(local_queries, HEADS, per_head)
    attention = (exponent / jnp.sum(exponent, axis=2, keepdims=True)).reshape(
        local_queries, att_width
    )
    attn_rounded = attention.astype(jnp.bfloat16)
    sample_grad = times_transpose(out_grad[0], out_weight).astype(jnp.bfloat16)
    every_grad, every_attn = (
        lax.all_gather(sample_grad, ("tile", "query"), axis=0, tiled=True),
        lax.all_gather(attn_rounded, ("tile", "query"), axis=0, tiled=True),
    )
    projected = jnp.dot(features[0], value_weight, preferred_element_type=jnp.float32).astype(
        jnp.bfloat16
    )
    token_count = projected.shape[0]
    capacity = slot_point.shape[1]
    points = slot_point[0]
    alive_slot = jnp.arange(capacity, dtype=jnp.int32) < slot_count[0, 0]
    query_index = points // att_width
    attn_column = points % att_width
    head_index = attn_column // per_head
    query_match = query_index[:, None] == jnp.arange(all_queries, dtype=jnp.int32)[None, :]
    query_onehot = query_match.astype(jnp.bfloat16)
    column_match = attn_column[:, None] == jnp.arange(att_width, dtype=jnp.int32)[None, :]
    attn_rows = jnp.dot(query_onehot, every_attn, preferred_element_type=jnp.float32)
    picked_attn = jnp.sum(jnp.where(column_match, attn_rows, jnp.zeros((), jnp.float32)), axis=1)
    weight = jnp.where(alive_slot, picked_attn, jnp.zeros((), jnp.float32))
    head_mask = jnp.arange(width, dtype=jnp.int32)[None, :] // head_width == head_index[:, None]
    grad_rows = jnp.dot(query_onehot, every_grad, preferred_element_type=jnp.float32)
    slot_grad = jnp.where(head_mask, grad_rows, jnp.zeros((), jnp.float32))
    offsets = (0, 1, TILE_W, TILE_W + 1)
    padded = jnp.concatenate([projected, jnp.zeros((TILE_W + 1, width), jnp.bfloat16)], axis=0)
    corner_table = jnp.concatenate(
        [padded[offset : offset + token_count] for offset in offsets], axis=1
    )
    base_row = slot_rows[0, 0]
    picked_all = corner_table[base_row].astype(jnp.float32)
    mixed_rows = jnp.zeros((capacity, width), jnp.float32)
    corner_dots = jnp.zeros((capacity,), jnp.float32)
    contributions = []
    for corner in range(4):
        bilinear = slot_bilinear[0, corner]
        picked = picked_all[:, corner * width : (corner + 1) * width]
        mixed_rows = mixed_rows + bilinear[:, None] * picked
        corner_dots = corner_dots + bilinear * jnp.sum(picked * slot_grad, axis=1)
        contributions.append((weight * bilinear)[:, None] * slot_grad)
    corner_sums = (
        jnp.zeros((token_count, 4 * width), jnp.float32)
        .at[base_row]
        .add(jnp.concatenate(contributions, axis=1))
    )
    value_grad = corner_sums[:, 0:width]
    for corner in range(1, 4):
        value_grad = value_grad + shift_down(
            corner_sums[:, corner * width : (corner + 1) * width], offsets[corner]
        )
    query_float = query_match.astype(jnp.float32)
    sampled_part = over_rows_exact(
        query_float, jnp.where(head_mask, weight[:, None] * mixed_rows, jnp.zeros((), jnp.float32))
    )
    dots_table = jnp.where(
        jnp.logical_and(column_match, alive_slot[:, None]),
        corner_dots[:, None],
        jnp.zeros((), jnp.float32),
    )
    attn_part = over_rows_exact(query_float, dots_table)
    sampled_share, attn_grad = (
        lax.psum_scatter(sampled_part, ("tile", "query"), scatter_dimension=0, tiled=True),
        lax.psum_scatter(attn_part, ("tile", "query"), scatter_dimension=0, tiled=True),
    )
    out_term = over_rows_exact(sampled_share, out_grad[0].astype(jnp.float32))
    attn_three = attention.reshape(local_queries, HEADS, per_head)
    grad_three = attn_grad.reshape(local_queries, HEADS, per_head)
    logit_grad = (
        (attn_three * (grad_three - jnp.sum(attn_three * grad_three, axis=2, keepdims=True)))
        .reshape(local_queries, att_width)
        .astype(jnp.bfloat16)
    )
    query_grad = times_transpose(logit_grad, attn_weight).astype(jnp.bfloat16)
    value_rounded = value_grad.astype(jnp.bfloat16)
    feature_grad = times_transpose(value_rounded, value_weight).astype(jnp.bfloat16)
    value_term = over_rows(features[0], value_rounded)
    attn_term = over_rows(queries[0], logit_grad)
    summed = lax.psum((value_term, attn_term, out_term), ("tile", "query", "dp"))
    return (
        feature_grad[None],
        query_grad[None],
        summed[0] * grad_scale,
        summed[1] * grad_scale,
        summed[2] * grad_scale,
    )


def solution(mesh):
    in_specs = (
        P("dp", ("tile", "query"), None),
        P("dp", ("tile", "query"), None),
        P("dp", ("tile", "query"), None),
        P(),
        P(),
        P(),
        P("dp", ("tile", "query")),
        P("dp", None, ("tile", "query")),
        P("dp", None, ("tile", "query")),
        P("dp", ("tile", "query")),
    )
    out_specs = (P("dp", ("tile", "query"), None), P("dp", ("tile", "query"), None), P(), P(), P())
    return jax.shard_map(local, mesh=mesh, in_specs=in_specs, out_specs=out_specs, check_vma=False)
```

profile of v0, /device:TPU:0, one launch (start us, length us, event | category | flops | bytes accessed | tf_op | source)
XLA Modules:
  0.0 305.3 jit_solution(8465550287204873643)
XLA Ops:
  7.2 0.0 copy-start
  7.2 0.0 reduce-scatter.2.cloned.1.call-start
  8.0 0.8 compare_select_fusion.2
  8.8 0.7 add_select_fusion.2
  9.5 1.0 convolution_exponential_fusion
  10.5 0.1 reshape.239
  10.6 0.1 reduce_sum.63
  10.7 0.1 div.48
  10.8 0.1 div.49
  10.9 10.4 %all_gather.6 = bf16[64,128]{1,0:T(8,128)(2,1)S(1)} all-gather(bf16[8,128]{1,0:T(8,128)(2,1)S(1)} %divide_convert_fusion), channel_id=1, replica_groups=mesh['tile'=4,'query'=2,'dp'=4] {'tile','query'}, dimensions={0}, use_global_device_ids=true | all-gather | bytes 18432 | tf_op jit(solution)/shard_map/all_gather | solution.py:69
  21.2 0.9 fusion.64
  22.2 0.0 copy-done
  22.2 1.6 convolution_convert_fusion
  23.8 1.3 pad_slice_fusion.2
  25.1 3.9 %pad_maximum_fusion.1 = bf16[4096,1024]{1,0:T(8,128)(2,1)} fusion(bf16[4096,256]{1,0:T(8,128)(2,1)S(1)} %get-tuple-element.35, bf16[4096,256]{1,0:T(8,128)(2,1)S(1)} %get-tuple-element.34, bf16[4096,256]{1,0:T(8,128)(2,1)S(1)} %get-tuple-element.33, bf16[4096,256]{1,0:T(8,128)(2,1)S(1)} %convolution_convert_fusion), kind=kLoop, calls=%fused_computation.4 | loop fusion | flops 33554432 | bytes 16777216 | tf_op jit(solution)/shard_map/concatenate | solution.py:92
  29.0 15.5 %gather_fusion = bf16[2048,1024]{1,0:T(8,128)(2,1)} fusion(bf16[4096,1024]{1,0:T(8,128)(2,1)} %pad_maximum_fusion.1, s32[2048]{0:T(1024)S(1)} %broadcast_clamp_fusion), kind=kCustom, calls=%fused_computation | custom fusion | bytes 8396800 | tf_op jit(solution)/shard_map/gather | solution.py:96
  44.5 6.5 %copy.27 = bf16[2048,1024]{0,1:T(8,128)(2,1)} copy(bf16[2048,1024]{1,0:T(8,128)(2,1)} %gather_fusion) | data formatting | bytes 8388608 | tf_op jit(solution)/shard_map/gather | solution.py:96
  51.0 3.3 %convert_element_type.32 = f32[2048,1024]{0,1:T(8,128)S(1)} convert(bf16[2048,1024]{0,1:T(8,128)(2,1)} %copy.27) | non-fusion elementwise | flops 2097152 | bytes 12582912 | tf_op jit(solution)/shard_map/convert_element_type | solution.py:96
  54.3 0.0 copy-start.2
  54.3 0.6 fusion.23
  54.9 2.6 copy-done.2
  57.5 0.0 copy-start.5
  57.5 2.7 fusion.7
  60.1 0.0 reduce-scatter.2.cloned.1.call-update
  60.2 0.0 all-reduce.8.cloned.1.call-start
  60.2 0.0 copy-done.5
  60.2 0.0 copy-done.6
  60.3 0.1 convolution_convert_fusion.3
  60.4 9.3 %all_gather.7 = bf16[64,256]{1,0:T(8,128)(2,1)S(1)} all-gather(bf16[8,256]{1,0:T(8,128)(2,1)S(1)} %convolution_convert_fusion.3), channel_id=1, replica_groups=mesh['tile'=4,'query'=2,'dp'=4] {'tile','query'}, dimensions={0}, use_global_device_ids=true | all-gather | bytes 36864 | tf_op jit(solution)/shard_map/all_gather | solution.py:68
  69.7 4.4 %multiply_reduce_fusion.3 = (f32[2048]{0:T(1024)S(1)}, f32[2048]{0:T(1024)S(1)}, f32[2048]{0:T(1024)S(1)}, f32[2048]{0:T(1024)S(1)}, f32[2048,256]{0,1:T(8,128)S...) fusion(f32[2048,1024]{0,1:T(8,128)} %copy-done.2, ...), kind=kOutput, calls=%fused_computation.32 | convolution fusion | flops 74571776 | bytes 16892928 | tf_op jit(solution)/shard_map/dot_general | solution.py:88
  74.0 3.8 %pad_maximum_fusion = f32[2048,1024]{0,1:T(8,128)} fusion(f32[2048,256]{0,1:T(8,128)S(1)} %get-tuple-element.29, f32[2048,256]{0,1:T(8,128)S(1)} %get-tuple-element.30, f32[2048,256]{0,1:T(8,128)S(1)} %get-tuple-element.31, f32[2048,256]{0,1:T(8,128)S(1)} %get-tuple-element.32), kind=kLoop, calls=%fused_computation.3 | loop fusion | flops 6291456 | bytes 16777216 | tf_op jit(solution)/shard_map/concatenate | solution.py:109
  77.8 9.3 %copy.26 = f32[2048,1024]{1,0:T(8,128)} copy(f32[2048,1024]{0,1:T(8,128)} %pad_maximum_fusion) | data formatting | bytes 16777216 | tf_op jit(solution)/shard_map/concatenate | solution.py:109
  87.1 25.7 %scatter_custom_fusion = f32[4096,1024]{1,0:T(8,128)} fusion(s32[2048]{0:T(1024)S(1)} %bitcast.62, f32[2048,1024]{1,0:T(8,128)} %copy.26, f32[]{:T(128)} %constant.54.clone.1), kind=kCustom, calls=%fused_computation.5 | custom fusion | flops 2097152 | bytes 16777728 | tf_op jit(solution)/shard_map/scatter-add | solution.py:109
  112.8 4.4 %slice.75 = f32[4031,256]{1,0:T(8,128)} slice(f32[4096,1024]{1,0:T(8,128)} %scatter_custom_fusion), slice={[0:4031], [768:1024]} | slice | bytes 8255488 | tf_op jit(solution)/shard_map/slice | solution.py:34
  117.2 4.4 %slice.74 = f32[4032,256]{1,0:T(8,128)} slice(f32[4096,1024]{1,0:T(8,128)} %scatter_custom_fusion), slice={[0:4032], [512:768]} | slice | bytes 8257536 | tf_op jit(solution)/shard_map/slice | solution.py:34
  121.6 4.4 %slice.73 = f32[4095,256]{1,0:T(8,128)} slice(f32[4096,1024]{1,0:T(8,128)} %scatter_custom_fusion), slice={[0:4095], [256:512]} | slice | bytes 8386560 | tf_op jit(solution)/shard_map/slice | solution.py:34
  126.0 1.3 fusion.33
  127.3 23.6 %all-reduce.4 = f32[64,128]{1,0:T(8,128)S(1)} all-reduce(f32[64,128]{1,0:T(8,128)S(1)} %fusion.33), channel_id=2, replica_groups=mesh['tile'=4,'query'=2,'dp'=4] {'tile','query'}, use_global_device_ids=true, to_apply=%region_7.8.clone | all-reduce | flops 8192 | bytes 65536
  151.0 0.0 copy-done.8
  151.0 0.6 dynamic-slice
  152.2 0.1 reshape.240
  152.3 1.2 fusion
  153.5 0.1 sub.31
  153.6 7.0 %fusion.6 = bf16[4096,256]{1,0:T(8,128)(2,1)S(1)} fusion(f32[4096,1024]{1,0:T(8,128)} %scatter_custom_fusion, f32[4031,256]{1,0:T(8,128)} %slice.75, f32[4032,256]{1,0:T(8,128)} %slice.74, f32[4095,256]{1,0:T(8,128)} %slice.73), kind=kLoop, calls=%fused_computation.13 | loop fusion | flops 4194304 | bytes 18741248 | tf_op jit(solution)/shard_map/convert_element_type | solution.py:139
  160.6 0.0 copy-start.1
  160.6 0.0 copy-start.7
  160.6 0.0 copy-start.4
  160.6 0.0 copy-start.3
  160.6 1.4 fusion.24
  162.1 0.0 copy-done.1
  162.1 0.0 copy-done.7
  162.1 0.9 convolution_bitcast_fusion
  163.0 1.7 fusion.56
  164.7 0.0 all-reduce.8.cloned.1.call-update
  164.7 0.0 copy-done.4
  164.7 0.7 fusion.27
  165.5 0.0 copy-done.3
  165.5 3.7 %fusion.3 = bf16[1,4096,256]{2,1,0:T(8,128)(2,1)} fusion(bf16[4096,256]{1,0:T(8,128)(2,1)} %copy-done.1, bf16[256,256]{1,0:T(8,128)(2,1)S(1)} %copy-done.3), kind=kOutput, calls=%fused_computation.9 | convolution fusion | flops 537919488 | bytes 4325376 | tf_op jit(solution)/shard_map/dot_general | solution.py:27
  169.1 124.9 %all-reduce.8.cloned.1.call-done = (f32[256,256]{0,1:T(8,128)}, f32[256,128]{0,1:T(8,128)}, f32[256,256]{0,1:T(8,128)}) async-done(((f32[256,256]{0,1:T(8,128)}, f32[256,128]{0,1:T(8,128)}, f32[256,256]{0,1:T(8,128)}), (f32[256,256]{0,1:T(8,128)}, f32[256,128]{0,1:T(8,128)}, f32[256,256]{0,1:T(8,128)})) %all-reduce.8.cloned.1.call-update) | async-done | bytes 655376 | tf_op jit(solution)/shard_map/psum | solution.py:143
  294.1 1.1 broadcast_multiply_fusion.4
  295.1 0.8 copy.31
  296.0 0.9 broadcast_multiply_fusion.6
  296.9 0.8 copy.30
  297.6 0.8 copy.29
  (12 shorter events, 0.1 us)
Async XLA Ops:
  7.2 15.0 %copy-start = (bf16[1,4096,256]{2,1,0:T(8,128)(2,1)S(1)}, bf16[1,4096,256]{2,1,0:T(8,128)(2,1)}, u32[]{:S(2)}) copy-start(bf16[1,4096,256]{2,1,0:T(8,128)(2,1)} %param.10) | copy-start | bytes 6291460
  7.2 155.8 %reduce-scatter.2.cloned.1.call-start = ((), (), s32[]{:S(2)}) async-start(), calls=%async_computation.1 | async-start | bytes 73728 | tf_op jit(solution)/shard_map/reduce_scatter | solution.py:127
  54.3 3.2 %copy-start.2 = (f32[2048,1024]{0,1:T(8,128)}, f32[2048,1024]{0,1:T(8,128)S(1)}, u32[]{:S(2)}) copy-start(f32[2048,1024]{0,1:T(8,128)S(1)} %convert_element_type.32) | copy-start | bytes 25165828
  57.5 2.8 copy-start.5
  57.5 2.8 copy-start.6
  60.2 233.9 %all-reduce.8.cloned.1.call-start = ((), (), s32[]{:S(2)}) async-start(), calls=%async_computation.2 | async-start | bytes 1310720 | tf_op jit(solution)/shard_map/psum | solution.py:143
  121.6 29.3 %copy-start.8 = (u32[32]{0:T(128)S(1)}, u32[32]{0:T(128)}, u32[]{:S(2)}) copy-start(u32[32]{0:T(128)} %constant.85) | copy-start | bytes 388
  160.6 1.5 copy-start.1
  160.6 1.5 copy-start.7
  160.6 4.1 %copy-start.4 = (bf16[256,128]{1,0:T(8,128)(2,1)S(1)}, bf16[256,128]{1,0:T(8,128)(2,1)}, u32[]{:S(2)}) copy-start(bf16[256,128]{1,0:T(8,128)(2,1)} %param.14) | copy-start | bytes 196612
  160.6 4.8 %copy-start.3 = (bf16[256,256]{1,0:T(8,128)(2,1)S(1)}, bf16[256,256]{1,0:T(8,128)(2,1)}, u32[]{:S(2)}) copy-start(bf16[256,256]{1,0:T(8,128)(2,1)} %param.13) | copy-start | bytes 393220
Sparse Core Ops, SparseCore 0:
  60.3 33.5 reduce-scatter.1
  164.8 129.1 all-reduce.7
where the time goes:
time: 306 us; the launch traced here: 305 us
  waiting for transfers between devices  125 us (41%)
  local copies, waits for them, and re-layouts  52.7 us (17%)
  other arithmetic  48.5 us (16%)
  blocking collectives  43.2 us (14%)
  matrix products  20.1 us (7%)
  between operations  15.7 us (5%)
    psum x1, waiting for transfers between devices, local(): lax.psum((value_term, attn_term, out_term), ('tile', 'query', 'dp'))  125 us
    scatter-add x1, other arithmetic, local(): corner_sums = jnp.zeros((token_count, 4 * width), jnp.float32).at[base_ro...  25.7 us
    unnamed x1, blocking collectives  23.6 us
    gather x2, local copies, waits for them, and re-layouts, local(): picked_all = corner_table[base_row].astype(jnp.float32)  22 us
    slice x3, local copies, waits for them, and re-layouts, shift_down(): block[:block.shape[0] - offset]  13.2 us
    all_gather x1, blocking collectives, local(): lax.all_gather(attn_rounded, ('tile', 'query'), axis=0, tiled=True)  10.4 us
    concatenate x1, local copies, waits for them, and re-layouts, local(): jnp.concatenate(contributions, axis=1)  9.28 us
    all_gather x1, blocking collectives, local(): lax.all_gather(sample_grad, ('tile', 'query'), axis=0, tiled=True)  9.25 us
  transfers between devices with their start and end apart: 2, of which 1 were waited for; matrix products, arithmetic and copies ran while one was open for 24% of the time, Pallas kernels for 0%

commit v1 on v0

v1 whole, which is shorter than its diff:
```python
import jax
import jax.numpy as jnp
from jax import lax
from jax.experimental import pallas as pl
from jax.experimental.pallas import tpu as pltpu
from jax.sharding import PartitionSpec as P

HEADS = 8
TILE_W = 64
MESH = pl.DeviceIdType.MESH
PAGE = ("tile", "query")


def dot(left, right, contract):
    return lax.dot_general(
        left, right, ((contract[:1], contract[1:]), ((), ())), preferred_element_type=jnp.float32
    )


def page_peer(offset):
    count = lax.axis_size(PAGE)
    cores = lax.axis_size("query")
    me = lax.axis_index("tile") * cores + lax.axis_index("query")
    peer = lax.rem(me + offset, count)
    return peer, {"tile": peer // cores, "query": lax.rem(peer, cores)}


def dp_peer(offset):
    return {"dp": lax.rem(lax.axis_index("dp") + offset, lax.axis_size("dp"))}


def greet(with_dp):
    barrier = pltpu.get_barrier_semaphore()
    count = lax.axis_size(PAGE)
    pages = lax.axis_size("dp") if with_dp else 1
    for offset in range(1, count):
        pl.semaphore_signal(barrier, inc=1, device_id=page_peer(offset)[1], device_id_type=MESH)
    for offset in range(1, pages):
        pl.semaphore_signal(barrier, inc=1, device_id=dp_peer(offset), device_id_type=MESH)
    pl.semaphore_wait(barrier, count - 1 + pages - 1)


def gather_kernel(mine_ref, every_ref, local_sem, send_sem, recv_sem):
    count = lax.axis_size(PAGE)
    me, _ = page_peer(0)
    greet(False)
    keep = pltpu.make_async_copy(mine_ref, every_ref.at[me], local_sem)
    keep.start()
    copies = []
    for offset in range(1, count):
        _, device = page_peer(offset)
        copy = pltpu.make_async_remote_copy(
            src_ref=mine_ref,
            dst_ref=every_ref.at[me],
            send_sem=send_sem.at[offset],
            recv_sem=recv_sem.at[offset],
            device_id=device,
            device_id_type=MESH,
        )
        copy.start()
        copies.append(copy)
    keep.wait()
    for copy in copies:
        copy.wait()


def page_kernel(
    count_ref,
    features_ref,
    queries_ref,
    out_grad_ref,
    value_weight_ref,
    attn_weight_ref,
    out_weight_ref,
    point_ref,
    rows_ref,
    bilinear_ref,
    feature_grad_ref,
    sums_ref,
    logit_ref,
    upper,
    lower,
    wrapped,
    corner_map,
    mixed,
    contribution,
    query_onehot,
    weight_row,
    value_total,
):
    step = pl.program_id(0)
    steps = pl.num_programs(0)
    width = value_weight_ref.shape[0]
    att_width = attn_weight_ref.shape[1]
    per_head = att_width // HEADS
    head_width = width // HEADS
    capacity = point_ref.shape[1]
    all_queries = queries_ref.shape[0]
    chunk = features_ref.shape[0]
    f32, bf16 = jnp.float32, jnp.bfloat16
    points = point_ref[...]
    column = lax.rem(points, att_width)
    head = column // per_head
    base = rows_ref[0:1, :]

    def head_mask():
        row = lax.broadcasted_iota(jnp.int32, (width, capacity), 0)
        return row // head_width == head

    def grad_rows():
        sample_grad = dot(out_weight_ref[...], out_grad_ref[...], (1, 1)).astype(bf16)
        return dot(sample_grad, query_onehot[...], (1, 0))

    def attention_of():
        exponent = jnp.exp(dot(queries_ref[...], attn_weight_ref[...], (1, 0)))
        return exponent / head_sum(exponent)

    def head_sum(values):
        same = (
            lax.broadcasted_iota(jnp.int32, (att_width, att_width), 0) // per_head
            == lax.broadcasted_iota(jnp.int32, (att_width, att_width), 1) // per_head
        )
        return lax.dot_general(
            values,
            jnp.where(same, 1.0, 0.0).astype(f32),
            (((1,), (0,)), ((), ())),
            precision=lax.Precision.HIGHEST,
            preferred_element_type=f32,
        )

    @pl.when(step == 0)
    def _():
        x = lax.rem(base, TILE_W)
        lane = lax.broadcasted_iota(jnp.int32, (TILE_W, capacity), 0)
        here, beside = lane == x, lane == x + 1
        over = jnp.logical_and(x == TILE_W - 1, lane == 0)
        b0, b1 = bilinear_ref[0:1, :], bilinear_ref[1:2, :]
        b2, b3 = bilinear_ref[2:3, :], bilinear_ref[3:4, :]
        zero = jnp.zeros((), f32)
        upper[...] = (jnp.where(here, b0, zero) + jnp.where(beside, b1, zero)).astype(bf16)
        lower[...] = (
            jnp.where(here, b2, zero) + jnp.where(beside, b3, zero) + jnp.where(over, b1, zero)
        ).astype(bf16)
        wrapped[...] = jnp.where(over, b3, zero)[0:16].astype(bf16)
        which = lax.broadcasted_iota(jnp.int32, (all_queries, capacity), 0)
        query_onehot[...] = jnp.where(which == points // att_width, 1.0, 0.0).astype(bf16)
        attn_rows = dot(attention_of().astype(bf16), query_onehot[...], (0, 0))
        attn_lane = lax.broadcasted_iota(jnp.int32, (att_width, capacity), 0)
        picked = jnp.sum(jnp.where(attn_lane == column, attn_rows, zero), axis=0, keepdims=True)
        slot = lax.broadcasted_iota(jnp.int32, (1, capacity), 1)
        weight = jnp.where(slot < count_ref[0, 0], picked, zero)
        weight_row[...] = weight
        spread = jnp.where(head_mask(), grad_rows() * weight, zero)
        contribution[...] = spread.T.astype(bf16)

    line = base // TILE_W
    for index in range(chunk // TILE_W):
        here = line - (step * (chunk // TILE_W) + index)

        def mask(shift):
            one = jnp.where(here == -shift, 1.0, 0.0).astype(f32)
            return jnp.broadcast_to(one, (16, capacity)).astype(bf16)

        first, second, third = mask(0), mask(1), mask(2)
        for part in range(TILE_W // 16):
            rows = slice(part * 16, part * 16 + 16)
            block = upper[rows] * first + lower[rows] * second
            if part == 0:
                block = block + wrapped[...] * third
            corner_map[index * TILE_W + part * 16 : index * TILE_W + part * 16 + 16, :] = block

    projected = dot(value_weight_ref[...], features_ref[...], (0, 1)).astype(bf16)
    added = dot(projected, corner_map[...], (1, 0))

    @pl.when(step == 0)
    def _():
        mixed[...] = added

    @pl.when(step > 0)
    def _():
        mixed[...] += added

    value_rounded = dot(corner_map[...], contribution[...], (1, 0)).astype(bf16)
    feature_grad_ref[...] = dot(value_rounded, value_weight_ref[...], (1, 1)).astype(bf16)
    term = dot(features_ref[...], value_rounded, (0, 0))

    @pl.when(step == 0)
    def _():
        value_total[...] = term

    @pl.when(step > 0)
    def _():
        value_total[...] += term

    @pl.when(step == steps - 1)
    def _():
        zero = jnp.zeros((), f32)
        own = jnp.where(head_mask(), mixed[...], zero)
        dots = jnp.sum(own * grad_rows(), axis=0, keepdims=True)
        slot = lax.broadcasted_iota(jnp.int32, (1, capacity), 1)
        dots = jnp.where(slot < count_ref[0, 0], dots, zero)
        attn_lane = lax.broadcasted_iota(jnp.int32, (att_width, capacity), 0)
        table = jnp.where(attn_lane == column, dots, zero)
        high = table.astype(bf16)
        low = (table - high.astype(f32)).astype(bf16)
        attn_grad = dot(query_onehot[...], high, (1, 1)) + dot(query_onehot[...], low, (1, 1))
        attention = attention_of()
        logit = attention * (attn_grad - head_sum(attention * attn_grad))
        logit_ref[...] = logit
        sampled = dot((own * weight_row[...]).astype(bf16), query_onehot[...], (1, 1))
        sampled_high = sampled.astype(bf16)
        sampled_low = (sampled - sampled_high.astype(f32)).astype(bf16)
        out_grad = out_grad_ref[...]
        kind = sums_ref.dtype
        sums_ref[:, 0:width] = value_total[...].astype(kind)
        sums_ref[:, width : 2 * width] = (
            dot(sampled_high, out_grad, (1, 0)) + dot(sampled_low, out_grad, (1, 0))
        ).astype(kind)
        sums_ref[:, 2 * width :] = dot(queries_ref[...], logit.astype(bf16), (0, 0)).astype(kind)


def sum_kernel(
    sums_ref,
    logit_ref,
    attn_weight_ref,
    total_ref,
    query_grad_ref,
    from_page,
    from_dp,
    from_logit,
    page_send,
    page_recv,
    logit_send,
    logit_recv,
    dp_send,
    dp_recv,
    all_send,
    all_recv,
):
    count = lax.axis_size(PAGE)
    pages = lax.axis_size("dp")
    me, _ = page_peer(0)
    f32 = jnp.float32
    kind = sums_ref.dtype
    greet(True)

    def remote(source, target, send, recv, offset, device):
        copy = pltpu.make_async_remote_copy(
            src_ref=source,
            dst_ref=target,
            send_sem=send.at[offset],
            recv_sem=recv.at[offset],
            device_id=device,
            device_id_type=MESH,
        )
        copy.start()
        return copy

    page_copies, logit_copies = [], []
    for offset in range(1, count):
        peer, device = page_peer(offset)
        page_copies.append(
            remote(sums_ref.at[peer], from_page.at[offset], page_send, page_recv, offset, device)
        )
    for offset in range(1, count):
        peer, device = page_peer(offset)
        logit_copies.append(
            remote(
                logit_ref.at[peer], from_logit.at[offset], logit_send, logit_recv, offset, device
            )
        )
    total = sums_ref[me].astype(f32)
    for offset in range(1, count):
        page_copies[offset - 1].wait()
        total = total + from_page[offset].astype(f32)
    from_dp[0] = total.astype(kind)
    dp_copies = []
    for offset in range(1, pages):
        dp_copies.append(
            remote(from_dp.at[0], from_dp.at[offset], dp_send, dp_recv, offset, dp_peer(offset))
        )
    logit = logit_ref[me]
    for offset in range(1, count):
        logit_copies[offset - 1].wait()
        logit = logit + from_logit[offset]
    query_grad_ref[...] = dot(
        logit.astype(jnp.bfloat16), attn_weight_ref[...], (1, 1)
    ).astype(jnp.bfloat16)
    for offset in range(1, pages):
        dp_copies[offset - 1].wait()
    total = from_dp[0].astype(f32)
    if pages > 1:
        mine = lax.axis_index("dp")
        total = jnp.zeros_like(total)
        for page in range(pages):
            total = total + from_dp[lax.rem(mine + pages - page, pages)].astype(f32)
    total_ref[me] = total.astype(kind)
    all_copies = []
    for offset in range(1, count):
        _, device = page_peer(offset)
        all_copies.append(
            remote(total_ref.at[me], total_ref.at[me], all_send, all_recv, offset, device)
        )
    for copy in all_copies:
        copy.wait()


def whole(shape):
    return pl.BlockSpec(shape, lambda step: (0,) * len(shape))


def local(
    features,
    queries,
    out_grad,
    value_weight,
    attn_weight,
    out_weight,
    slot_point,
    slot_rows,
    slot_bilinear,
    slot_count,
):
    owners = lax.axis_size(PAGE)
    page_count = lax.axis_size("dp")
    local_queries = queries.shape[1]
    all_queries = local_queries * owners
    grad_scale = float(page_count * all_queries) ** (-0.5)
    tokens, width = features.shape[1:]
    att_width = attn_weight.shape[1]
    capacity = slot_point.shape[1]
    f32, bf16 = jnp.float32, jnp.bfloat16
    vmem = pl.BlockSpec(memory_space=pltpu.VMEM)
    dma = pltpu.SemaphoreType.DMA

    every = pl.pallas_call(
        gather_kernel,
        out_shape=jax.ShapeDtypeStruct((owners, 2 * local_queries, width), bf16),
        in_specs=[vmem],
        out_specs=vmem,
        scratch_shapes=[dma, dma((owners,)), dma((owners,))],
        compiler_params=pltpu.CompilerParams(collective_id=0, has_side_effects=True),
    )(jnp.concatenate([queries[0], out_grad[0]], axis=0))
    every_query = every[:, :local_queries].reshape(all_queries, width)
    every_out = every[:, local_queries:].reshape(all_queries, width)

    sum_width = 2 * width + att_width
    sum_rows = width // owners
    kind = bf16 if sum_rows % 16 == 0 else f32
    chunk = 512
    feature_grad, sums, logit = pl.pallas_call(
        page_kernel,
        grid=(tokens // chunk,),
        out_shape=(
            jax.ShapeDtypeStruct((tokens, width), bf16),
            jax.ShapeDtypeStruct((width, sum_width), kind),
            jax.ShapeDtypeStruct((all_queries, att_width), f32),
        ),
        in_specs=[
            pl.BlockSpec(memory_space=pltpu.SMEM),
            pl.BlockSpec((chunk, width), lambda step: (step, 0)),
            whole((all_queries, width)),
            whole((all_queries, width)),
            whole((width, width)),
            whole((width, att_width)),
            whole((width, width)),
            whole((1, capacity)),
            whole((4, capacity)),
            whole((4, capacity)),
        ],
        out_specs=(
            pl.BlockSpec((chunk, width), lambda step: (step, 0)),
            whole((width, sum_width)),
            whole((all_queries, att_width)),
        ),
        scratch_shapes=[
            pltpu.VMEM((TILE_W, capacity), bf16),
            pltpu.VMEM((TILE_W, capacity), bf16),
            pltpu.VMEM((16, capacity), bf16),
            pltpu.VMEM((chunk, capacity), bf16),
            pltpu.VMEM((width, capacity), f32),
            pltpu.VMEM((capacity, width), bf16),
            pltpu.VMEM((all_queries, capacity), bf16),
            pltpu.VMEM((1, capacity), f32),
            pltpu.VMEM((width, width), f32),
        ],
        compiler_params=pltpu.CompilerParams(vmem_limit_bytes=48 * 1024 * 1024),
    )(
        slot_count,
        features[0],
        every_query,
        every_out,
        value_weight,
        attn_weight,
        out_weight,
        slot_point,
        slot_rows[0],
        slot_bilinear[0],
    )

    total, query_grad = pl.pallas_call(
        sum_kernel,
        out_shape=(
            jax.ShapeDtypeStruct((owners, sum_rows, sum_width), kind),
            jax.ShapeDtypeStruct((local_queries, width), bf16),
        ),
        in_specs=[vmem] * 3,
        out_specs=(vmem, vmem),
        scratch_shapes=[
            pltpu.VMEM((owners, sum_rows, sum_width), kind),
            pltpu.VMEM((page_count, sum_rows, sum_width), kind),
            pltpu.VMEM((owners, local_queries, att_width), f32),
            dma((owners,)),
            dma((owners,)),
            dma((owners,)),
            dma((owners,)),
            dma((page_count,)),
            dma((page_count,)),
            dma((owners,)),
            dma((owners,)),
        ],
        compiler_params=pltpu.CompilerParams(
            collective_id=1, has_side_effects=True, vmem_limit_bytes=32 * 1024 * 1024
        ),
    )(
        sums.reshape(owners, sum_rows, sum_width),
        logit.reshape(owners, local_queries, att_width),
        attn_weight,
    )
    total = total.reshape(width, sum_width)
    return (
        feature_grad[None],
        query_grad[None],
        total[:, :width].astype(f32) * grad_scale,
        total[:, 2 * width :].astype(f32) * grad_scale,
        total[:, width : 2 * width].astype(f32) * grad_scale,
    )


def solution(mesh):
    in_specs = (
        P("dp", ("tile", "query"), None),
        P("dp", ("tile", "query"), None),
        P("dp", ("tile", "query"), None),
        P(),
        P(),
        P(),
        P("dp", ("tile", "query")),
        P("dp", None, ("tile", "query")),
        P("dp", None, ("tile", "query")),
        P("dp", ("tile", "query")),
    )
    out_specs = (P("dp", ("tile", "query"), None), P("dp", ("tile", "query"), None), P(), P(), P())
    return jax.shard_map(local, mesh=mesh, in_specs=in_specs, out_specs=out_specs, check_vma=False)
```

time: 306 us -> 62.1 us (0.20)
  waiting for transfers between devices: 125 us -> 0 us
  Pallas kernels: 0 us -> 49.4 us
  other arithmetic: 48.5 us -> 2.8 us
  local copies, waits for them, and re-layouts: 52.7 us -> 7.82 us
  blocking collectives: 43.2 us -> 0 us
  matrix products: 20.1 us -> 0 us
  between operations: 15.7 us -> 1.3 us
    psum x1 -> x0, waiting for transfers between devices: 125 us -> none  [local(): lax.psum((value_term, attn_term, out_term), ('tile', 'query', 'dp'))]
    pallas_call x0 -> x3, Pallas kernels: none -> 49.4 us  [the longest x1 22.6 us: local(): pl.pallas_call(page_kernel, grid=(tokens // chunk,), out_shape=(jax.Shape...]
    scatter-add x1 -> x0, other arithmetic: 25.7 us -> none  [local(): corner_sums = jnp.zeros((token_count, 4 * width), jnp.float32).at[base_ro...]
    unnamed x1 -> x0, blocking collectives: 23.6 us -> none
    gather x2 -> x0, local copies, waits for them, and re-layouts: 22 us -> none  [local(): picked_all = corner_table[base_row].astype(jnp.float32)]
    dot_general x12 -> x0, matrix products: 20.1 us -> none  [the longest x3 5.68 us: over_rows_exact(): lax.dot_general(left, right, (((0,), (0,)), ((), ())), precision=lax.Prec...]
    all_gather x2 -> x0, blocking collectives: 19.6 us -> none  [the longest x1 10.4 us: local(): lax.all_gather(attn_rounded, ('tile', 'query'), axis=0, tiled=True)]
    slice x5 -> x0, local copies, waits for them, and re-layouts: 15.4 us -> none  [the longest x3 13.2 us: shift_down(): block[:block.shape[0] - offset]]
  transfers between devices with their start and end apart: 2 -> 0, of which waited for: 1 -> 0; matrix products, arithmetic and copies ran while one was open for 24% -> 0% of each run, Pallas kernels for 0% -> 0%
where the time goes in v1:
time: 62.1 us; the launch traced here: 61.4 us
  Pallas kernels  49.4 us (80%)
  local copies, waits for them, and re-layouts  7.82 us (13%)
  other arithmetic  2.8 us (5%)
  between operations  1.3 us (2%)
    pallas_call x1, Pallas kernels, local(): pl.pallas_call(page_kernel, grid=(tokens // chunk,), out_shape=(jax.Shape...  22.6 us
    pallas_call x1, Pallas kernels, local(): pl.pallas_call(sum_kernel, out_shape=(jax.ShapeDtypeStruct((owners, sum_r...  19.1 us
    pallas_call x1, Pallas kernels, local(): pl.pallas_call(gather_kernel, out_shape=jax.ShapeDtypeStruct((owners, 2 *...  7.74 us
    unnamed x15, local copies, waits for them, and re-layouts  7.04 us
    concatenate x1, other arithmetic, local(): jnp.concatenate([queries[0], out_grad[0]], axis=0)  1.3 us

profile of v1, /device:TPU:0, one launch (start us, length us, event | category | flops | bytes accessed | tf_op | source)
XLA Modules:
  0.0 61.4 jit_solution(17569268509913218256)
XLA Ops:
  1.3 1.3 %pad_maximum_fusion.mine_ref = bf16[16,256]{1,0:T(8,128)(2,1)} fusion(bf16[8,256]{1,0:T(8,128)(2,1)} %bitcast.22, bf16[8,256]{1,0:T(8,128)(2,1)} %bitcast.23), kind=kLoop, calls=%fused_computation.5 | loop fusion | flops 16384 | bytes 16384 | tf_op jit(solution)/shard_map/concatenate | solution.py:343
  2.6 7.7 %shard_map.137 = bf16[8,16,256]{2,1,0:T(8,128)(2,1)} custom-call(bf16[16,256]{1,0:T(8,128)(2,1)} %pad_maximum_fusion.mine_ref), custom_call_target="tpu_custom_call" | custom-call | tf_op jit(solution)/shard_map/pallas_call | solution.py:336
  10.3 0.8 %slice_bitcast_fusion = (bf16[64,256]{1,0:T(8,128)(2,1)S(1)}, bf16[64,256]{1,0:T(8,128)(2,1)S(1)}) fusion(bf16[8,16,256]{2,1,0:T(8,128)(2,1)} %shard_map.137), kind=kLoop, calls=%fused_computation.3 | loop fusion | bytes 131072 | tf_op jit(solution)/shard_map/reshape | solution.py:345
  11.1 0.0 copy-start
  11.1 1.6 %copy-done = bf16[1,4096,256]{2,1,0:T(8,128)(2,1)S(1)} copy-done((bf16[1,4096,256]{2,1,0:T(8,128)(2,1)S(1)}, bf16[1,4096,256]{2,1,0:T(8,128)(2,1)}, u32[]{:S(2)}) %copy-start) | copy-done | bytes 2097176
  12.7 0.0 copy-start.1
  12.7 0.8 %copy-done.1 = bf16[256,128]{1,0:T(8,128)(2,1)S(1)} copy-done((bf16[256,128]{1,0:T(8,128)(2,1)S(1)}, bf16[256,128]{1,0:T(8,128)(2,1)}, u32[]{:S(2)}) %copy-start.1) | copy-done | bytes 65560
  13.5 0.0 copy-start.2
  13.5 0.9 %copy-done.2 = bf16[256,256]{1,0:T(8,128)(2,1)S(1)} copy-done((bf16[256,256]{1,0:T(8,128)(2,1)S(1)}, bf16[256,256]{1,0:T(8,128)(2,1)}, u32[]{:S(2)}) %copy-start.2) | copy-done | bytes 131096
  14.4 0.0 copy-start.3
  14.4 0.9 %copy-done.3 = bf16[256,256]{1,0:T(8,128)(2,1)S(1)} copy-done((bf16[256,256]{1,0:T(8,128)(2,1)S(1)}, bf16[256,256]{1,0:T(8,128)(2,1)}, u32[]{:S(2)}) %copy-start.3) | copy-done | bytes 131096
  15.4 0.0 copy-start.4
  15.4 0.8 %copy-done.4 = s32[1,4,2048]{2,1,0:T(4,128)S(1)} copy-done((s32[1,4,2048]{2,1,0:T(4,128)S(1)}, s32[1,4,2048]{2,1,0:T(4,128)}, u32[]{:S(2)}) %copy-start.4) | copy-done | bytes 32792
  16.1 0.0 copy-start.5
  16.1 0.8 %copy-done.5 = f32[1,4,2048]{2,1,0:T(4,128)S(1)} copy-done((f32[1,4,2048]{2,1,0:T(4,128)S(1)}, f32[1,4,2048]{2,1,0:T(4,128)}, u32[]{:S(2)}) %copy-start.5) | copy-done | bytes 32792
  16.9 0.0 copy-start.6
  16.9 0.7 %copy-done.6 = s32[1,2048]{1,0:T(1,128)S(1)} copy-done((s32[1,2048]{1,0:T(1,128)S(1)}, s32[1,2048]{1,0:T(1,128)}, u32[]{:S(2)}) %copy-start.6) | copy-done | bytes 8216
  17.6 22.6 %shard_map.138 = (bf16[4096,256]{1,0:T(8,128)(2,1)}, bf16[256,640]{1,0:T(8,128)(2,1)S(1)}, f32[64,128]{1,0:T(8,128)S(1)}) custom-call(s32[1,1]{1,0:T(1,128)S(6)} %copy.16.count_ref, bf16[4096,256]{1,0:T(8,128)(2,1)S(1)} %bitcast.14, bf16[64,256]{1,0:T(8,128)(2,1)S(1)} %get-tuple-element.18.queries_ref, bf16[64,256]{1,0:T(8,128)(2,1)S(1)} %get-tuple-element.17.out_grad_ref, ...), custom_call_target="tpu_custom_call" | custom-call | tf_op jit(solution)/shard_map/pallas_call | solution.py:351
  40.2 19.1 %shard_map.139 = (bf16[8,32,640]{2,1,0:T(8,128)(2,1)S(1)}, bf16[8,256]{1,0:T(8,128)(2,1)S(1)}) custom-call(bf16[8,32,640]{2,1,0:T(8,128)(2,1)S(1)} %bitcast.17, f32[8,8,128]{2,1,0:T(8,128)S(1)} %bitcast.20, bf16[256,128]{1,0:T(8,128)(2,1)S(1)} %copy-done.1), custom_call_target="tpu_custom_call" | custom-call | tf_op jit(solution)/shard_map/pallas_call | solution.py:401
  59.3 0.7 %convert_multiply_fusion.2 = f32[256,128]{1,0:T(8,128)} fusion(bf16[256,640]{1,0:T(8,128)(2,1)S(1)} %bitcast.15), kind=kLoop, calls=%fused_computation.2 | loop fusion | flops 65536 | bytes 196608 | tf_op jit(solution)/shard_map/mul | solution.py:435
  59.9 0.8 %convert_multiply_fusion = (f32[256,256]{1,0:T(8,128)}, f32[256,256]{1,0:T(8,128)}) fusion(bf16[256,640]{1,0:T(8,128)(2,1)S(1)} %bitcast.16), kind=kLoop, calls=%fused_computation | loop fusion | flops 262144 | bytes 786432 | tf_op jit(solution)/shard_map/mul | solution.py:436
  60.8 0.6 copy.17
Async XLA Ops:
  11.1 1.6 %copy-start = (bf16[1,4096,256]{2,1,0:T(8,128)(2,1)S(1)}, bf16[1,4096,256]{2,1,0:T(8,128)(2,1)}, u32[]{:S(2)}) copy-start(bf16[1,4096,256]{2,1,0:T(8,128)(2,1)} %param.10) | copy-start | bytes 6291460
  12.7 0.8 %copy-start.1 = (bf16[256,128]{1,0:T(8,128)(2,1)S(1)}, bf16[256,128]{1,0:T(8,128)(2,1)}, u32[]{:S(2)}) copy-start(bf16[256,128]{1,0:T(8,128)(2,1)} %attn_weight_ref.3) | copy-start | bytes 196612
  13.5 0.9 %copy-start.2 = (bf16[256,256]{1,0:T(8,128)(2,1)S(1)}, bf16[256,256]{1,0:T(8,128)(2,1)}, u32[]{:S(2)}) copy-start(bf16[256,256]{1,0:T(8,128)(2,1)} %value_weight_ref.1) | copy-start | bytes 393220
  14.4 0.9 %copy-start.3 = (bf16[256,256]{1,0:T(8,128)(2,1)S(1)}, bf16[256,256]{1,0:T(8,128)(2,1)}, u32[]{:S(2)}) copy-start(bf16[256,256]{1,0:T(8,128)(2,1)} %out_weight_ref.1) | copy-start | bytes 393220
  15.4 0.8 %copy-start.4 = (s32[1,4,2048]{2,1,0:T(4,128)S(1)}, s32[1,4,2048]{2,1,0:T(4,128)}, u32[]{:S(2)}) copy-start(s32[1,4,2048]{2,1,0:T(4,128)} %param.17) | copy-start | bytes 98308
  16.1 0.8 %copy-start.5 = (f32[1,4,2048]{2,1,0:T(4,128)S(1)}, f32[1,4,2048]{2,1,0:T(4,128)}, u32[]{:S(2)}) copy-start(f32[1,4,2048]{2,1,0:T(4,128)} %param.18) | copy-start | bytes 98308
  16.9 0.7 %copy-start.6 = (s32[1,2048]{1,0:T(1,128)S(1)}, s32[1,2048]{1,0:T(1,128)}, u32[]{:S(2)}) copy-start(s32[1,2048]{1,0:T(1,128)} %point_ref.1) | copy-start | bytes 24580

commit v2 on v0

v2 whole, which is shorter than its diff:
```python
import jax
import jax.numpy as jnp
from jax import lax
from jax.experimental import pallas as pl
from jax.experimental.pallas import tpu as pltpu
from jax.sharding import PartitionSpec as P

HEADS = 8
TILE_W = 64
MESH = pl.DeviceIdType.MESH
PAGE = ("tile", "query")
CHUNK = 512


def dot(left, right, contract):
    return lax.dot_general(
        left, right, ((contract[:1], contract[1:]), ((), ())), preferred_element_type=jnp.float32
    )


def page_peer(offset):
    count = lax.axis_size(PAGE)
    cores = lax.axis_size("query")
    me = lax.axis_index("tile") * cores + lax.axis_index("query")
    peer = lax.rem(me + offset, count)
    return peer, {"tile": peer // cores, "query": lax.rem(peer, cores)}


def dp_peer(offset):
    return {"dp": lax.rem(lax.axis_index("dp") + offset, lax.axis_size("dp"))}


def greet():
    barrier = pltpu.get_barrier_semaphore()
    count = lax.axis_size(PAGE)
    pages = lax.axis_size("dp")
    for offset in range(1, count):
        pl.semaphore_signal(barrier, inc=1, device_id=page_peer(offset)[1], device_id_type=MESH)
    for offset in range(1, pages):
        pl.semaphore_signal(barrier, inc=1, device_id=dp_peer(offset), device_id_type=MESH)
    pl.semaphore_wait(barrier, count - 1 + pages - 1)


def remote(source, target, sems, offset, device):
    copy = pltpu.make_async_remote_copy(
        src_ref=source,
        dst_ref=target,
        send_sem=sems.at[0, offset],
        recv_sem=sems.at[1, offset],
        device_id=device,
        device_id_type=MESH,
    )
    copy.start()
    return copy


class Exchange:
    def __init__(self, mine, from_page, from_dp, total, page_sems, dp_sems, all_sems):
        self.mine, self.from_page, self.from_dp, self.total = mine, from_page, from_dp, total
        self.page_sems, self.dp_sems, self.all_sems = page_sems, dp_sems, all_sems
        self.count, self.pages = lax.axis_size(PAGE), lax.axis_size("dp")

    def send_page(self):
        self.copies = []
        for offset in range(1, self.count):
            peer, device = page_peer(offset)
            target = self.from_page.at[offset]
            self.copies.append(
                remote(self.mine.at[peer], target, self.page_sems, offset, device)
            )

    def send_dp(self):
        me, _ = page_peer(0)
        total = self.mine[me].astype(jnp.float32)
        for offset in range(1, self.count):
            self.copies[offset - 1].wait()
            total = total + self.from_page[offset].astype(jnp.float32)
        self.from_dp[0] = total.astype(self.from_dp.dtype)
        self.copies = []
        for offset in range(1, self.pages):
            target = self.from_dp.at[offset]
            self.copies.append(
                remote(self.from_dp.at[0], target, self.dp_sems, offset, dp_peer(offset))
            )

    def send_all(self):
        me, _ = page_peer(0)
        for copy in self.copies:
            copy.wait()
        mine = lax.axis_index("dp")
        total = jnp.zeros(self.mine.shape[1:], jnp.float32)
        for page in range(self.pages):
            source = lax.rem(mine + self.pages - page, self.pages)
            total = total + self.from_dp[source].astype(jnp.float32)
        self.total[me] = total.astype(self.total.dtype)
        self.copies = []
        for offset in range(1, self.count):
            _, device = page_peer(offset)
            self.copies.append(
                remote(self.total.at[me], self.total.at[me], self.all_sems, offset, device)
            )

    def finish(self):
        for copy in self.copies:
            copy.wait()


def page_kernel(
    count_ref,
    features_hbm,
    query_ref,
    grad_ref,
    value_weight_ref,
    attn_weight_ref,
    out_weight_ref,
    point_ref,
    rows_ref,
    bilinear_ref,
    feature_grad_hbm,
    query_grad_ref,
    early_total,
    late_total,
    features,
    feature_grad,
    packed,
    every,
    upper,
    lower,
    wrapped,
    corner_map,
    mixed,
    grad_rows,
    contribution,
    query_onehot,
    value_total,
    early,
    early_page,
    early_dp,
    late,
    late_page,
    late_dp,
    logit_parts,
    from_logit,
    local_sem,
    in_sems,
    out_sems,
    gather_sems,
    logit_sems,
    early_page_sems,
    early_dp_sems,
    early_all_sems,
    late_page_sems,
    late_dp_sems,
    late_all_sems,
):
    f32, bf16 = jnp.float32, jnp.bfloat16
    owners = lax.axis_size(PAGE)
    me, _ = page_peer(0)
    width = value_weight_ref.shape[0]
    att_width = attn_weight_ref.shape[1]
    per_head = att_width // HEADS
    head_width = width // HEADS
    capacity = point_ref.shape[1]
    local_queries = query_ref.shape[0]
    all_queries = local_queries * owners
    tokens = features.shape[0]
    chunk = CHUNK
    steps = tokens // chunk
    zero = jnp.zeros((), f32)

    def rows_of(index):
        return pl.ds(pl.multiple_of(index * chunk, chunk), chunk)

    def copy_in(index):
        rows = rows_of(index)
        return pltpu.make_async_copy(features_hbm.at[rows], features.at[rows], in_sems.at[index])

    def copy_out(index):
        rows = rows_of(index)
        return pltpu.make_async_copy(
            feature_grad.at[rows], feature_grad_hbm.at[rows], out_sems.at[index]
        )

    @pl.loop(0, steps)
    def _(index):
        copy_in(index).start()

    packed[...] = jnp.concatenate(
        [query_ref[...].astype(f32), grad_ref[...].astype(f32)], axis=0
    ).astype(bf16)
    greet()
    keep = pltpu.make_async_copy(packed, every.at[me], local_sem)
    keep.start()
    gathers = []
    for offset in range(1, owners):
        _, device = page_peer(offset)
        gathers.append(remote(packed, every.at[me], gather_sems, offset, device))

    points = point_ref[...]
    column = lax.rem(points, att_width)
    head = lax.div(column, per_head)
    base = rows_ref[0:1, :]
    x = lax.rem(base, TILE_W)
    lane = lax.broadcasted_iota(jnp.int32, (TILE_W, capacity), 0)
    here, beside = lane == x, lane == x + 1
    over = jnp.logical_and(x == TILE_W - 1, lane == 0)
    b0, b1 = bilinear_ref[0:1, :], bilinear_ref[1:2, :]
    b2, b3 = bilinear_ref[2:3, :], bilinear_ref[3:4, :]
    upper[...] = (jnp.where(here, b0, zero) + jnp.where(beside, b1, zero)).astype(bf16)
    lower[...] = (
        jnp.where(here, b2, zero) + jnp.where(beside, b3, zero) + jnp.where(over, b1, zero)
    ).astype(bf16)
    wrapped[...] = jnp.where(over, b3, zero)[0:16].astype(bf16)
    which = lax.broadcasted_iota(jnp.int32, (all_queries, capacity), 0)
    query_onehot[...] = jnp.where(which == lax.div(points, att_width), 1.0, 0.0).astype(bf16)
    mixed[...] = jnp.zeros_like(mixed)
    line = lax.div(base, TILE_W)

    @pl.loop(0, steps)
    def _(step):
        for index in range(chunk // TILE_W):
            ahead = line - (step * (chunk // TILE_W) + index)

            def mask(shift):
                one = jnp.where(ahead == -shift, 1.0, 0.0).astype(f32)
                return jnp.broadcast_to(one, (16, capacity)).astype(bf16)

            first, second, third = mask(0), mask(1), mask(2)
            for part in range(TILE_W // 16):
                rows = slice(part * 16, part * 16 + 16)
                block = upper[rows] * first + lower[rows] * second
                if part == 0:
                    block = block + wrapped[...] * third
                place = pl.multiple_of(step * chunk + index * TILE_W + part * 16, 16)
                corner_map[pl.ds(place, 16), :] = block
        copy_in(step).wait()
        rows = rows_of(step)
        projected = dot(value_weight_ref[...], features[rows], (0, 1)).astype(bf16)
        mixed[...] += dot(projected, corner_map[rows], (1, 0))

    keep.wait()
    for copy in gathers:
        copy.wait()
    everything = every[...].astype(f32)
    queries = everything[:, :local_queries].reshape(all_queries, width).astype(bf16)
    out_grad = everything[:, local_queries:].reshape(all_queries, width).astype(bf16)

    def head_sum(values):
        same = lax.div(
            lax.broadcasted_iota(jnp.int32, (att_width, att_width), 0), per_head
        ) == lax.div(lax.broadcasted_iota(jnp.int32, (att_width, att_width), 1), per_head)
        return lax.dot_general(
            values,
            jnp.where(same, 1.0, 0.0).astype(f32),
            (((1,), (0,)), ((), ())),
            precision=lax.Precision.HIGHEST,
            preferred_element_type=f32,
        )

    exponent = jnp.exp(dot(queries, attn_weight_ref[...], (1, 0)))
    attention = exponent / head_sum(exponent)
    attn_rows = dot(attention.astype(bf16), query_onehot[...], (0, 0))
    attn_lane = lax.broadcasted_iota(jnp.int32, (att_width, capacity), 0)
    picked = jnp.sum(jnp.where(attn_lane == column, attn_rows, zero), axis=0, keepdims=True)
    alive = lax.broadcasted_iota(jnp.int32, (1, capacity), 1) < count_ref[0, 0]
    weight = jnp.where(alive, picked, zero)
    sample_grad = dot(out_weight_ref[...], out_grad, (1, 1)).astype(bf16)
    grad_rows[...] = dot(sample_grad, query_onehot[...], (1, 0))
    dots = jnp.zeros((1, capacity), f32)
    for index in range(HEADS):
        rows = slice(index * head_width, (index + 1) * head_width)
        match = head == index
        block, pulled = grad_rows[rows], mixed[rows]
        dots = dots + jnp.where(match, jnp.sum(block * pulled, axis=0, keepdims=True), zero)
        scaled = jnp.where(match, weight, zero)
        contribution[:, rows] = (block * scaled).astype(bf16).T
        mixed[rows] = pulled * scaled
    dots = jnp.where(alive, dots, zero)
    table = jnp.where(attn_lane == column, dots, zero)
    high = table.astype(bf16)
    low = (table - high.astype(f32)).astype(bf16)
    attn_grad = dot(query_onehot[...], high, (1, 1)) + dot(query_onehot[...], low, (1, 1))
    logit = attention * (attn_grad - head_sum(attention * attn_grad))
    logit_parts[...] = logit.reshape(logit_parts.shape)
    logit_copies = []
    for offset in range(1, owners):
        peer, device = page_peer(offset)
        logit_copies.append(
            remote(logit_parts.at[peer], from_logit.at[offset], logit_sems, offset, device)
        )
    sampled = dot(mixed[...].astype(bf16), query_onehot[...], (1, 1))
    sampled_high = sampled.astype(bf16)
    sampled_low = (sampled - sampled_high.astype(f32)).astype(bf16)
    out_term = dot(sampled_high, out_grad, (1, 0)) + dot(sampled_low, out_grad, (1, 0))
    attn_term = dot(queries, logit.astype(bf16), (0, 0))
    kind = early.dtype
    per_owner = early.shape[:2]
    early[:, :, :width] = out_term.reshape(per_owner + (width,)).astype(kind)
    early[:, :, width:] = attn_term.reshape(per_owner + (att_width,)).astype(kind)
    early_sum = Exchange(
        early, early_page, early_dp, early_total, early_page_sems, early_dp_sems, early_all_sems
    )
    late_sum = Exchange(
        late, late_page, late_dp, late_total, late_page_sems, late_dp_sems, late_all_sems
    )
    early_sum.send_page()
    value_total[...] = jnp.zeros_like(value_total)

    def value_steps(first, last):
        @pl.loop(first, last)
        def _(step):
            rows = rows_of(step)
            value_rounded = dot(corner_map[rows], contribution[...], (1, 0)).astype(bf16)
            value_total[...] += dot(features[rows], value_rounded, (0, 0))
            feature_grad[rows] = dot(value_rounded, value_weight_ref[...], (1, 1)).astype(bf16)
            copy_out(step).start()

    value_steps(0, steps // 2)
    early_sum.send_dp()
    value_steps(steps // 2, steps)
    late[...] = value_total[...].reshape(late.shape).astype(kind)
    late_sum.send_page()
    early_sum.send_all()
    total = logit_parts[me]
    for offset in range(1, owners):
        logit_copies[offset - 1].wait()
        total = total + from_logit[offset]
    query_grad_ref[...] = dot(total.astype(bf16), attn_weight_ref[...], (1, 1)).astype(bf16)
    late_sum.send_dp()
    early_sum.finish()
    late_sum.send_all()

    @pl.loop(0, steps)
    def _(index):
        copy_out(index).wait()

    late_sum.finish()


def local(
    features,
    queries,
    out_grad,
    value_weight,
    attn_weight,
    out_weight,
    slot_point,
    slot_rows,
    slot_bilinear,
    slot_count,
):
    owners = lax.axis_size(PAGE)
    page_count = lax.axis_size("dp")
    local_queries = queries.shape[1]
    all_queries = local_queries * owners
    grad_scale = float(page_count * all_queries) ** (-0.5)
    tokens, width = features.shape[1:]
    att_width = attn_weight.shape[1]
    capacity = slot_point.shape[1]
    f32, bf16 = jnp.float32, jnp.bfloat16
    vmem = pl.BlockSpec(memory_space=pltpu.VMEM)
    dma = pltpu.SemaphoreType.DMA

    any_space = pl.BlockSpec(memory_space=pl.ANY)
    rows = width // owners
    kind = bf16 if rows % 16 == 0 else f32
    early_width = width + att_width
    steps = tokens // CHUNK
    feature_grad, query_grad, early, late = pl.pallas_call(
        page_kernel,
        out_shape=(
            jax.ShapeDtypeStruct((tokens, width), bf16),
            jax.ShapeDtypeStruct((local_queries, width), bf16),
            jax.ShapeDtypeStruct((owners, rows, early_width), kind),
            jax.ShapeDtypeStruct((owners, rows, width), kind),
        ),
        in_specs=[pl.BlockSpec(memory_space=pltpu.SMEM), any_space] + [vmem] * 8,
        out_specs=(any_space, vmem, vmem, vmem),
        scratch_shapes=[
            pltpu.VMEM((tokens, width), bf16),
            pltpu.VMEM((tokens, width), bf16),
            pltpu.VMEM((2 * local_queries, width), bf16),
            pltpu.VMEM((owners, 2 * local_queries, width), bf16),
            pltpu.VMEM((TILE_W, capacity), bf16),
            pltpu.VMEM((TILE_W, capacity), bf16),
            pltpu.VMEM((16, capacity), bf16),
            pltpu.VMEM((tokens, capacity), bf16),
            pltpu.VMEM((width, capacity), f32),
            pltpu.VMEM((width, capacity), f32),
            pltpu.VMEM((capacity, width), bf16),
            pltpu.VMEM((all_queries, capacity), bf16),
            pltpu.VMEM((width, width), f32),
            pltpu.VMEM((owners, rows, early_width), kind),
            pltpu.VMEM((owners, rows, early_width), kind),
            pltpu.VMEM((page_count, rows, early_width), kind),
            pltpu.VMEM((owners, rows, width), kind),
            pltpu.VMEM((owners, rows, width), kind),
            pltpu.VMEM((page_count, rows, width), kind),
            pltpu.VMEM((owners, local_queries, att_width), f32),
            pltpu.VMEM((owners, local_queries, att_width), f32),
            dma,
            dma((steps,)),
            dma((steps,)),
            dma((2, owners)),
            dma((2, owners)),
            dma((2, owners)),
            dma((2, page_count)),
            dma((2, owners)),
            dma((2, owners)),
            dma((2, page_count)),
            dma((2, owners)),
        ],
        compiler_params=pltpu.CompilerParams(
            collective_id=0, has_side_effects=True, vmem_limit_bytes=60 * 1024 * 1024
        ),
    )(
        slot_count,
        features[0],
        queries[0],
        out_grad[0],
        value_weight,
        attn_weight,
        out_weight,
        slot_point,
        slot_rows[0],
        slot_bilinear[0],
    )
    early = early.reshape(width, early_width)
    late = late.reshape(width, width)
    return (
        feature_grad[None],
        query_grad[None],
        late.astype(f32) * grad_scale,
        early[:, width:].astype(f32) * grad_scale,
        early[:, :width].astype(f32) * grad_scale,
    )


def solution(mesh):
    in_specs = (
        P("dp", ("tile", "query"), None),
        P("dp", ("tile", "query"), None),
        P("dp", ("tile", "query"), None),
        P(),
        P(),
        P(),
        P("dp", ("tile", "query")),
        P("dp", None, ("tile", "query")),
        P("dp", None, ("tile", "query")),
        P("dp", ("tile", "query")),
    )
    out_specs = (P("dp", ("tile", "query"), None), P("dp", ("tile", "query"), None), P(), P(), P())
    return jax.shard_map(local, mesh=mesh, in_specs=in_specs, out_specs=out_specs, check_vma=False)
```

time: 306 us -> 55.9 us (0.18)
  waiting for transfers between devices: 125 us -> 0 us
  local copies, waits for them, and re-layouts: 52.7 us -> 3.64 us
  Pallas kernels: 0 us -> 46 us
  other arithmetic: 48.5 us -> 4.76 us
  blocking collectives: 43.2 us -> 0 us
  matrix products: 20.1 us -> 0 us
  between operations: 15.7 us -> 1.29 us
    psum x1 -> x0, waiting for transfers between devices: 125 us -> none  [local(): lax.psum((value_term, attn_term, out_term), ('tile', 'query', 'dp'))]
    pallas_call x0 -> x1, Pallas kernels: none -> 46 us  [local(): pl.pallas_call(page_kernel, out_shape=(jax.ShapeDtypeStruct((tokens, widt...]
    scatter-add x1 -> x0, other arithmetic: 25.7 us -> none  [local(): corner_sums = jnp.zeros((token_count, 4 * width), jnp.float32).at[base_ro...]
    unnamed x1 -> x0, blocking collectives: 23.6 us -> none
    gather x2 -> x0, local copies, waits for them, and re-layouts: 22 us -> none  [local(): picked_all = corner_table[base_row].astype(jnp.float32)]
    dot_general x12 -> x0, matrix products: 20.1 us -> none  [the longest x3 5.68 us: over_rows_exact(): lax.dot_general(left, right, (((0,), (0,)), ((), ())), precision=lax.Prec...]
    all_gather x2 -> x0, blocking collectives: 19.6 us -> none  [the longest x1 10.4 us: local(): lax.all_gather(attn_rounded, ('tile', 'query'), axis=0, tiled=True)]
    slice x5 -> x0, local copies, waits for them, and re-layouts: 15.4 us -> none  [the longest x3 13.2 us: shift_down(): block[:block.shape[0] - offset]]
  transfers between devices with their start and end apart: 2 -> 0, of which waited for: 1 -> 0; matrix products, arithmetic and copies ran while one was open for 24% -> 0% of each run, Pallas kernels for 0% -> 0%
where the time goes in v2:
time: 55.9 us; the launch traced here: 55.6 us
  Pallas kernels  46 us (82%)
  other arithmetic  4.76 us (9%)
  local copies, waits for them, and re-layouts  3.64 us (7%)
  between operations  1.29 us (2%)
    pallas_call x1, Pallas kernels, local(): pl.pallas_call(page_kernel, out_shape=(jax.ShapeDtypeStruct((tokens, widt...  46 us
    unnamed x4, local copies, waits for them, and re-layouts  3.64 us
    mul x1, other arithmetic, local(): late.astype(f32) * grad_scale  1.63 us
    mul x1, other arithmetic, local(): early[:, :width].astype(f32) * grad_scale  1.63 us
    mul x1, other arithmetic, local(): early[:, width:].astype(f32) * grad_scale  1.51 us

profile of v2, /device:TPU:0, one launch (start us, length us, event | category | flops | bytes accessed | tf_op | source)
XLA Modules:
  0.0 55.6 jit_solution(11233952198285039782)
XLA Ops:
  1.3 46.0 %shard_map.137 = (bf16[4096,256]{1,0:T(8,128)(2,1)}, bf16[8,256]{1,0:T(8,128)(2,1)}, bf16[8,32,384]{2,1,0:T(8,128)(2,1)}, bf16[8,32,256]{2,1,0:T(8,128)(2,1)}) custom-call(s32[1,1]{1,0:T(1,128)S(6)} %copy.17.count_ref, bf16[4096,256]{1,0:T(8,128)(2,1)} %bitcast.9, bf16[8,256]{1,0:T(8,128)(2,1)} %bitcast.16, bf16[8,256]{1,0:T(8,128)(2,1)} %bitcast.17, ...), custom_call_target="tpu_custom_call" | custom-call | tf_op jit(solution)/shard_map/pallas_call | solution.py:369
  47.2 1.5 %convert_multiply_fusion.2 = f32[256,128]{1,0:T(8,128)} fusion(bf16[256,384]{1,0:T(8,128)(2,1)} %bitcast.12), kind=kLoop, calls=%fused_computation.2 | loop fusion | flops 65536 | bytes 196608 | tf_op jit(solution)/shard_map/mul | solution.py:434
  48.7 1.6 %convert_multiply_fusion = f32[256,256]{1,0:T(8,128)} fusion(bf16[256,384]{1,0:T(8,128)(2,1)} %bitcast.13), kind=kLoop, calls=%fused_computation | loop fusion | flops 131072 | bytes 393216 | tf_op jit(solution)/shard_map/mul | solution.py:435
  50.4 1.6 %convert_multiply_fusion.1 = f32[8,32,256]{2,1,0:T(8,128)} fusion(bf16[8,32,256]{2,1,0:T(8,128)(2,1)} %get-tuple-element.11), kind=kLoop, calls=%fused_computation.1 | loop fusion | flops 131072 | bytes 393216 | tf_op jit(solution)/shard_map/mul | solution.py:433
  52.0 0.0 copy-start
  52.0 3.0 %copy.18 = bf16[1,4096,256]{2,1,0:T(8,128)(2,1)} copy(bf16[1,4096,256]{2,1,0:T(8,128)(2,1)} %bitcast.10) | data formatting | bytes 4194304
  55.1 0.0 copy-done
  55.1 0.6 %copy.19 = bf16[1,8,256]{2,1,0:T(8,128)(2,1)} copy(bf16[1,8,256]{2,1,0:T(8,128)(2,1)S(1)} %bitcast.18) | data formatting | bytes 8192
Async XLA Ops:
  52.0 3.0 %copy-start = (bf16[8,256]{1,0:T(8,128)(2,1)S(1)}, bf16[8,256]{1,0:T(8,128)(2,1)}, u32[]{:S(2)}) copy-start(bf16[8,256]{1,0:T(8,128)(2,1)} %get-tuple-element.10) | copy-start | bytes 12292

commit v3 on v2

--- a/solution.py
+++ b/solution.py
@@ -9,7 +9,7 @@
 TILE_W = 64
 MESH = pl.DeviceIdType.MESH
 PAGE = ("tile", "query")
-CHUNK = 512
+CHUNK = 1024
 
 
 def dot(left, right, contract):
@@ -30,7 +30,7 @@
     return {"dp": lax.rem(lax.axis_index("dp") + offset, lax.axis_size("dp"))}
 
 
-def greet():
+def greet_all():
     barrier = pltpu.get_barrier_semaphore()
     count = lax.axis_size(PAGE)
     pages = lax.axis_size("dp")
@@ -38,7 +38,11 @@
         pl.semaphore_signal(barrier, inc=1, device_id=page_peer(offset)[1], device_id_type=MESH)
     for offset in range(1, pages):
         pl.semaphore_signal(barrier, inc=1, device_id=dp_peer(offset), device_id_type=MESH)
-    pl.semaphore_wait(barrier, count - 1 + pages - 1)
+
+
+def await_all():
+    barrier = pltpu.get_barrier_semaphore()
+    pl.semaphore_wait(barrier, lax.axis_size(PAGE) + lax.axis_size("dp") - 2)
 
 
 def remote(source, target, sems, offset, device):
@@ -116,12 +120,16 @@
     point_ref,
     rows_ref,
     bilinear_ref,
-    feature_grad_hbm,
+    value_grad_hbm,
     query_grad_ref,
+    value_weight_grad,
+    out_weight_grad,
+    attn_weight_grad,
     early_total,
     late_total,
+    line_rows,
     features,
-    feature_grad,
+    value_grad,
     packed,
     every,
     upper,
@@ -178,24 +186,14 @@
     def copy_out(index):
         rows = rows_of(index)
         return pltpu.make_async_copy(
-            feature_grad.at[rows], feature_grad_hbm.at[rows], out_sems.at[index]
+            value_grad.at[rows], value_grad_hbm.at[rows], out_sems.at[index]
         )
 
     @pl.loop(0, steps)
     def _(index):
         copy_in(index).start()
 
-    packed[...] = jnp.concatenate(
-        [query_ref[...].astype(f32), grad_ref[...].astype(f32)], axis=0
-    ).astype(bf16)
-    greet()
-    keep = pltpu.make_async_copy(packed, every.at[me], local_sem)
-    keep.start()
-    gathers = []
-    for offset in range(1, owners):
-        _, device = page_peer(offset)
-        gathers.append(remote(packed, every.at[me], gather_sems, offset, device))
-
+    greet_all()
     points = point_ref[...]
     column = lax.rem(points, att_width)
     head = lax.div(column, per_head)
@@ -216,27 +214,47 @@
     mixed[...] = jnp.zeros_like(mixed)
     line = lax.div(base, TILE_W)
 
-    @pl.loop(0, steps)
-    def _(step):
-        for index in range(chunk // TILE_W):
-            ahead = line - (step * (chunk // TILE_W) + index)
-
-            def mask(shift):
-                one = jnp.where(ahead == -shift, 1.0, 0.0).astype(f32)
-                return jnp.broadcast_to(one, (16, capacity)).astype(bf16)
-
-            first, second, third = mask(0), mask(1), mask(2)
-            for part in range(TILE_W // 16):
-                rows = slice(part * 16, part * 16 + 16)
-                block = upper[rows] * first + lower[rows] * second
-                if part == 0:
-                    block = block + wrapped[...] * third
-                place = pl.multiple_of(step * chunk + index * TILE_W + part * 16, 16)
-                corner_map[pl.ds(place, 16), :] = block
-        copy_in(step).wait()
-        rows = rows_of(step)
-        projected = dot(value_weight_ref[...], features[rows], (0, 1)).astype(bf16)
-        mixed[...] += dot(projected, corner_map[rows], (1, 0))
+    line_rows[...] = jnp.broadcast_to(line.astype(f32), (16, capacity)).astype(bf16)
+
+    def sample_steps(start, stop):
+        @pl.loop(start, stop)
+        def _(step):
+            def mask(index):
+                number = (step * (chunk // TILE_W) + index).astype(f32)
+                return line_rows[...] == jnp.full((16, capacity), number, f32).astype(bf16)
+
+            none = jnp.zeros((16, capacity), bf16)
+            second, third = mask(-1), mask(-2)
+            for index in range(chunk // TILE_W):
+                first = mask(index)
+                for part in range(TILE_W // 16):
+                    rows = slice(part * 16, part * 16 + 16)
+                    block = none
+                    if part == 0:
+                        block = jnp.where(third, wrapped[...], block)
+                    block = jnp.where(second, lower[rows], block)
+                    block = jnp.where(first, upper[rows], block)
+                    place = pl.multiple_of(step * chunk + index * TILE_W + part * 16, 16)
+                    corner_map[pl.ds(place, 16), :] = block
+                second, third = first, second
+            copy_in(step).wait()
+            rows = rows_of(step)
+            projected = dot(value_weight_ref[...], features[rows], (0, 1)).astype(bf16)
+            mixed[...] += dot(projected, corner_map[rows], (1, 0))
+
+    sample_steps(0, steps // 2)
+    packed[...] = jnp.concatenate(
+        [query_ref[...].astype(f32), grad_ref[...].astype(f32)], axis=0
+    ).astype(bf16)
+    await_all()
+    keep = pltpu.make_async_copy(packed, every.at[me], local_sem)
+    keep.start()
+    gathers = []
+    for offset in range(1, owners):
+        _, device = page_peer(offset)
+        gathers.append(remote(packed, every.at[me], gather_sems, offset, device))
+
+    sample_steps(steps // 2, steps)
 
     keep.wait()
     for copy in gathers:
@@ -312,7 +330,7 @@
             rows = rows_of(step)
             value_rounded = dot(corner_map[rows], contribution[...], (1, 0)).astype(bf16)
             value_total[...] += dot(features[rows], value_rounded, (0, 0))
-            feature_grad[rows] = dot(value_rounded, value_weight_ref[...], (1, 1)).astype(bf16)
+            value_grad[rows] = value_rounded
             copy_out(step).start()
 
     value_steps(0, steps // 2)
@@ -329,12 +347,18 @@
     late_sum.send_dp()
     early_sum.finish()
     late_sum.send_all()
+    grad_scale = float(lax.axis_size("dp") * all_queries) ** (-0.5)
+    total = early_total[...].astype(f32) * grad_scale
+    out_weight_grad[...] = total[:, :, :width].reshape(width, width)
+    attn_weight_grad[...] = total[:, :, width:].reshape(width, att_width)
 
     @pl.loop(0, steps)
     def _(index):
         copy_out(index).wait()
 
     late_sum.finish()
+    total = late_total[...].astype(f32) * grad_scale
+    value_weight_grad[...] = total.reshape(width, width)
 
 
 def local(
@@ -353,7 +377,6 @@
     page_count = lax.axis_size("dp")
     local_queries = queries.shape[1]
     all_queries = local_queries * owners
-    grad_scale = float(page_count * all_queries) ** (-0.5)
     tokens, width = features.shape[1:]
     att_width = attn_weight.shape[1]
     capacity = slot_point.shape[1]
@@ -366,17 +389,21 @@
     kind = bf16 if rows % 16 == 0 else f32
     early_width = width + att_width
     steps = tokens // CHUNK
-    feature_grad, query_grad, early, late = pl.pallas_call(
+    value_grad, query_grad, late, out_grads, attn_grads = pl.pallas_call(
         page_kernel,
         out_shape=(
             jax.ShapeDtypeStruct((tokens, width), bf16),
             jax.ShapeDtypeStruct((local_queries, width), bf16),
-            jax.ShapeDtypeStruct((owners, rows, early_width), kind),
-            jax.ShapeDtypeStruct((owners, rows, width), kind),
+            jax.ShapeDtypeStruct((width, width), f32),
+            jax.ShapeDtypeStruct((width, width), f32),
+            jax.ShapeDtypeStruct((width, att_width), f32),
         ),
         in_specs=[pl.BlockSpec(memory_space=pltpu.SMEM), any_space] + [vmem] * 8,
-        out_specs=(any_space, vmem, vmem, vmem),
+        out_specs=(any_space, vmem, vmem, vmem, vmem),
         scratch_shapes=[
+            pltpu.VMEM((owners, rows, early_width), kind),
+            pltpu.VMEM((owners, rows, width), kind),
+            pltpu.VMEM((16, capacity), bf16),
             pltpu.VMEM((tokens, width), bf16),
             pltpu.VMEM((tokens, width), bf16),
             pltpu.VMEM((2 * local_queries, width), bf16),
@@ -425,15 +452,8 @@
         slot_rows[0],
         slot_bilinear[0],
     )
-    early = early.reshape(width, early_width)
-    late = late.reshape(width, width)
-    return (
-        feature_grad[None],
-        query_grad[None],
-        late.astype(f32) * grad_scale,
-        early[:, width:].astype(f32) * grad_scale,
-        early[:, :width].astype(f32) * grad_scale,
-    )
+    feature_grad = dot(value_grad, value_weight, (1, 1)).astype(bf16)
+    return feature_grad[None], query_grad[None], late, attn_grads, out_grads
 
 
 def solution(mesh):

time: 55.9 us -> 49.4 us (0.88)
  other arithmetic: 4.76 us -> 0 us
  Pallas kernels: 46 us -> 41.4 us
  matrix products: 0 us -> 3.71 us
  local copies, waits for them, and re-layouts: 3.64 us -> 2.67 us
    mul x3 -> x0, other arithmetic: 4.76 us -> none  [the longest x1 1.63 us: local(): late.astype(f32) * grad_scale]
    pallas_call x1, Pallas kernels: 46 us -> 41.4 us  [local(): pl.pallas_call(page_kernel, out_shape=(jax.ShapeDtypeStruct((tokens, widt...]
    dot_general x0 -> x1, matrix products: none -> 3.71 us  [dot(): lax.dot_general(left, right, ((contract[:1], contract[1:]), ((), ())), pr...]
    unnamed x4 -> x14, local copies, waits for them, and re-layouts: 3.64 us -> 2.67 us
where the time goes in v3:
time: 49.4 us; the launch traced here: 49.2 us
  Pallas kernels  41.4 us (84%)
  matrix products  3.71 us (8%)
  local copies, waits for them, and re-layouts  2.67 us (5%)
  between operations  1.38 us (3%)
    pallas_call x1, Pallas kernels, local(): pl.pallas_call(page_kernel, out_shape=(jax.ShapeDtypeStruct((tokens, widt...  41.4 us
    dot_general x1, matrix products, dot(): lax.dot_general(left, right, ((contract[:1], contract[1:]), ((), ())), pr...  3.71 us
    unnamed x14, local copies, waits for them, and re-layouts  2.67 us

profile of v3, /device:TPU:0, one launch (start us, length us, event | category | flops | bytes accessed | tf_op | source)
XLA Modules:
  0.0 49.2 jit_solution(213722926220444397)
XLA Ops:
  0.6 0.0 copy-start
  1.3 41.4 %shard_map.137 = (bf16[4096,256]{1,0:T(8,128)(2,1)}, bf16[8,256]{1,0:T(8,128)(2,1)}, f32[256,256]{1,0:T(8,128)}, f32[256,256]{1,0:T(8,128)}, f32[256,128]{1,0:T(8,128)}) custom-call(s32[1,1]{1,0:T(1,128)S(6)} %copy.19.count_ref, bf16[4096,256]{1,0:T(8,128)(2,1)} %bitcast.10, bf16[8,256]{1,0:T(8,128)(2,1)} %bitcast.13, bf16[8,256]{1,0:T(8,128)(2,1)} %bitcast.14, ...), custom_call_target="tpu_custom_call" | custom-call | tf_op jit(solution)/shard_map/pallas_call | solution.py:392
  42.8 0.0 copy-done
  42.8 0.0 copy-start.4
  42.8 0.0 copy-start.2
  42.8 0.0 copy-start.3
  42.8 0.0 copy-start.1
  42.8 3.7 %fusion = bf16[1,4096,256]{2,1,0:T(8,128)(2,1)} fusion(bf16[4096,256]{1,0:T(8,128)(2,1)} %get-tuple-element.10, bf16[256,256]{1,0:T(8,128)(2,1)S(1)} %copy-done), kind=kOutput, calls=%fused_computation.1 | convolution fusion | flops 537919488 | bytes 4325376 | tf_op jit(solution)/shard_map/dot_general | solution.py:16
  46.5 0.0 copy-done.4
  46.5 0.6 %copy.20 = bf16[1,8,256]{2,1,0:T(8,128)(2,1)} copy(bf16[1,8,256]{2,1,0:T(8,128)(2,1)S(1)} %bitcast.15) | data formatting | bytes 8192
  47.1 0.0 copy-done.2
  47.1 0.7 %copy.21 = f32[256,256]{1,0:T(8,128)} copy(f32[256,256]{1,0:T(8,128)S(1)} %copy-done.2) | data formatting | bytes 524288
  47.8 0.0 copy-done.3
  47.9 0.7 %copy.22 = f32[256,128]{1,0:T(8,128)} copy(f32[256,128]{1,0:T(8,128)S(1)} %copy-done.3) | data formatting | bytes 262144
  48.5 0.0 copy-done.1
  48.5 0.7 %copy.23 = f32[256,256]{1,0:T(8,128)} copy(f32[256,256]{1,0:T(8,128)S(1)} %copy-done.1) | data formatting | bytes 524288
Async XLA Ops:
  0.6 42.1 %copy-start = (bf16[256,256]{1,0:T(8,128)(2,1)S(1)}, bf16[256,256]{1,0:T(8,128)(2,1)}, u32[]{:S(2)}) copy-start(bf16[256,256]{1,0:T(8,128)(2,1)} %value_weight_ref.1) | copy-start | bytes 393220
  42.8 3.8 %copy-start.4 = (bf16[8,256]{1,0:T(8,128)(2,1)S(1)}, bf16[8,256]{1,0:T(8,128)(2,1)}, u32[]{:S(2)}) copy-start(bf16[8,256]{1,0:T(8,128)(2,1)} %get-tuple-element.11) | copy-start | bytes 12292
  42.8 4.3 %copy-start.2 = (f32[256,256]{1,0:T(8,128)S(1)}, f32[256,256]{1,0:T(8,128)}, u32[]{:S(2)}) copy-start(f32[256,256]{1,0:T(8,128)} %get-tuple-element.22) | copy-start | bytes 786436
  42.8 5.0 %copy-start.3 = (f32[256,128]{1,0:T(8,128)S(1)}, f32[256,128]{1,0:T(8,128)}, u32[]{:S(2)}) copy-start(f32[256,128]{1,0:T(8,128)} %get-tuple-element.23) | copy-start | bytes 393220
  42.8 5.7 %copy-start.1 = (f32[256,256]{1,0:T(8,128)S(1)}, f32[256,256]{1,0:T(8,128)}, u32[]{:S(2)}) copy-start(f32[256,256]{1,0:T(8,128)} %get-tuple-element.24) | copy-start | bytes 786436

commit v4 on v3

--- a/solution.py
+++ b/solution.py
@@ -1,3 +1,5 @@
+import functools
+
 import jax
 import jax.numpy as jnp
 from jax import lax
@@ -122,9 +124,6 @@
     bilinear_ref,
     value_grad_hbm,
     query_grad_ref,
-    value_weight_grad,
-    out_weight_grad,
-    attn_weight_grad,
     early_total,
     late_total,
     line_rows,
@@ -347,18 +346,43 @@
     late_sum.send_dp()
     early_sum.finish()
     late_sum.send_all()
-    grad_scale = float(lax.axis_size("dp") * all_queries) ** (-0.5)
-    total = early_total[...].astype(f32) * grad_scale
-    out_weight_grad[...] = total[:, :, :width].reshape(width, width)
-    attn_weight_grad[...] = total[:, :, width:].reshape(width, att_width)
 
     @pl.loop(0, steps)
     def _(index):
         copy_out(index).wait()
 
     late_sum.finish()
-    total = late_total[...].astype(f32) * grad_scale
-    value_weight_grad[...] = total.reshape(width, width)
+
+
+def last_kernel(
+    grad_scale,
+    value_grad_ref,
+    value_weight_ref,
+    query_ref,
+    early_ref,
+    late_ref,
+    feature_grad_ref,
+    query_grad_ref,
+    value_weight_grad,
+    attn_weight_grad,
+    out_weight_grad,
+):
+    feature_grad_ref[...] = dot(value_grad_ref[...], value_weight_ref[...], (1, 1)).astype(
+        jnp.bfloat16
+    )
+
+    @pl.when(pl.program_id(0) == 0)
+    def _():
+        width = value_weight_ref.shape[0]
+        query_grad_ref[...] = query_ref[...]
+        value_weight_grad[...] = late_ref[...].astype(jnp.float32) * grad_scale
+        early = early_ref[...].astype(jnp.float32) * grad_scale
+        out_weight_grad[...] = early[:, :width]
+        attn_weight_grad[...] = early[:, width:]
+
+
+def whole(shape):
+    return pl.BlockSpec(shape, lambda step: (0,) * len(shape))
 
 
 def local(
@@ -389,20 +413,17 @@
     kind = bf16 if rows % 16 == 0 else f32
     early_width = width + att_width
     steps = tokens // CHUNK
-    value_grad, query_grad, late, out_grads, attn_grads = pl.pallas_call(
+    value_grad, query_grad, early, late = pl.pallas_call(
         page_kernel,
         out_shape=(
             jax.ShapeDtypeStruct((tokens, width), bf16),
             jax.ShapeDtypeStruct((local_queries, width), bf16),
-            jax.ShapeDtypeStruct((width, width), f32),
-            jax.ShapeDtypeStruct((width, width), f32),
-            jax.ShapeDtypeStruct((width, att_width), f32),
+            jax.ShapeDtypeStruct((owners, rows, early_width), kind),
+            jax.ShapeDtypeStruct((owners, rows, width), kind),
         ),
         in_specs=[pl.BlockSpec(memory_space=pltpu.SMEM), any_space] + [vmem] * 8,
-        out_specs=(any_space, vmem, vmem, vmem, vmem),
+        out_specs=(any_space, vmem, vmem, vmem),
         scratch_shapes=[
-            pltpu.VMEM((owners, rows, early_width), kind),
-            pltpu.VMEM((owners, rows, width), kind),
             pltpu.VMEM((16, capacity), bf16),
             pltpu.VMEM((tokens, width), bf16),
             pltpu.VMEM((tokens, width), bf16),
@@ -452,8 +473,41 @@
         slot_rows[0],
         slot_bilinear[0],
     )
-    feature_grad = dot(value_grad, value_weight, (1, 1)).astype(bf16)
-    return feature_grad[None], query_grad[None], late, attn_grads, out_grads
+    grad_scale = float(page_count * all_queries) ** (-0.5)
+    block = pl.BlockSpec((CHUNK, width), lambda step: (step, 0))
+    feature_grad, query_grad, value_grads, attn_grads, out_grads = pl.pallas_call(
+        functools.partial(last_kernel, grad_scale),
+        grid=(steps,),
+        out_shape=(
+            jax.ShapeDtypeStruct((tokens, width), bf16),
+            jax.ShapeDtypeStruct((local_queries, width), bf16),
+            jax.ShapeDtypeStruct((width, width), f32),
+            jax.ShapeDtypeStruct((width, att_width), f32),
+            jax.ShapeDtypeStruct((width, width), f32),
+        ),
+        in_specs=[
+            block,
+            whole((width, width)),
+            whole((local_queries, width)),
+            whole((width, early_width)),
+            whole((width, width)),
+        ],
+        out_specs=(
+            block,
+            whole((local_queries, width)),
+            whole((width, width)),
+            whole((width, att_width)),
+            whole((width, width)),
+        ),
+        compiler_params=pltpu.CompilerParams(vmem_limit_bytes=60 * 1024 * 1024),
+    )(
+        value_grad,
+        value_weight,
+        query_grad,
+        early.reshape(width, early_width),
+        late.reshape(width, width),
+    )
+    return feature_grad[None], query_grad[None], value_grads, attn_grads, out_grads
 
 
 def solution(mesh):

time: 49.4 us -> 47.6 us (0.964)
  Pallas kernels: 41.4 us -> 46.1 us
  matrix products: 3.71 us -> 0 us
  local copies, waits for them, and re-layouts: 2.67 us -> 0 us
    pallas_call x0 -> x1, Pallas kernels: none -> 4.78 us  [local(): pl.pallas_call(functools.partial(last_kernel, grad_scale), grid=(steps,),...]
    dot_general x1 -> x0, matrix products: 3.71 us -> none  [dot(): lax.dot_general(left, right, ((contract[:1], contract[1:]), ((), ())), pr...]
    unnamed x14 -> x0, local copies, waits for them, and re-layouts: 2.67 us -> none
where the time goes in v4:
time: 47.6 us; the launch traced here: 47.4 us
  Pallas kernels  46.1 us (97%)
  between operations  1.29 us (3%)
    pallas_call x1, Pallas kernels, local(): pl.pallas_call(page_kernel, out_shape=(jax.ShapeDtypeStruct((tokens, widt...  41.3 us
    pallas_call x1, Pallas kernels, local(): pl.pallas_call(functools.partial(last_kernel, grad_scale), grid=(steps,),...  4.78 us

profile of v4, /device:TPU:0, one launch (start us, length us, event | category | flops | bytes accessed | tf_op | source)
XLA Modules:
  0.0 47.4 jit_solution(624650531904931001)
XLA Ops:
  1.3 41.3 %shard_map.137 = (bf16[4096,256]{1,0:T(8,128)(2,1)}, bf16[8,256]{1,0:T(8,128)(2,1)}, bf16[8,32,384]{2,1,0:T(8,128)(2,1)}, bf16[8,32,256]{2,1,0:T(8,128)(2,1)}) custom-call(s32[1,1]{1,0:T(1,128)S(6)} %copy.15.count_ref, bf16[4096,256]{1,0:T(8,128)(2,1)} %bitcast.9, bf16[8,256]{1,0:T(8,128)(2,1)} %bitcast.14, bf16[8,256]{1,0:T(8,128)(2,1)} %bitcast.15, ...), custom_call_target="tpu_custom_call" | custom-call | tf_op jit(solution)/shard_map/pallas_call | solution.py:416
  42.6 4.8 %shard_map.138 = (bf16[4096,256]{1,0:T(8,128)(2,1)}, bf16[8,256]{1,0:T(8,128)(2,1)}, f32[256,256]{1,0:T(8,128)}, f32[256,128]{1,0:T(8,128)}, f32[256,256]{1,0:T(8,128)}) custom-call(bf16[4096,256]{1,0:T(8,128)(2,1)} %get-tuple-element.14.value_grad_ref, bf16[256,256]{1,0:T(8,128)(2,1)} %value_weight_ref.3, bf16[8,256]{1,0:T(8,128)(2,1)} %get-tuple-element.15.query_ref, ...), custom_call_target="tpu_custom_call" | custom-call | tf_op jit(solution)/shard_map/pallas_call | solution.py:478
